TPU v7x, 32 devices: a whole 2x2x4 slice. The times are simulated.
32 devices in a mesh: parts: 2 (over y), lat: 4 (over z), height: 2 (over x), sub: 2 (over core).
Axes of the slice: x: 2, y: 2, z: 4, core: 2. Of those that a mesh axis runs over, the one named last changes fastest.
Arguments:
- thermal_excess_field: float32 [128, 16, 128], P(('parts', 'lat', 'sub'), 'height'), parts along dimension 0, may hold values from -6 to 6
- thermal_diffusivity: float32 [128, 16, 128], P(('parts', 'lat', 'sub'), 'height'), parts along dimension 0, may hold values from 0.1 to 0.9
- material_shift_field: float32 [3, 128, 16, 128], P(None, ('parts', 'lat', 'sub'), 'height'), parts along dimension 1, may hold values from -0.15 to 0.15
- stack_deposit_tally: int32 [128, 128], P('parts'), parts along dimension 0, may hold values from 4 to 16
- laser_target_sites: int32 [4, 128], P('parts'), parts along dimension 0, may hold values from 0 to 131071
Outputs:
- temperature_out: float32 [128, 16, 128], P(('parts', 'lat', 'sub'), 'height'), parts along dimension 0
- force: float32 [3, 128, 16, 128], P(None, ('parts', 'lat', 'sub'), 'height'), parts along dimension 1
There are 2 independent parts, one for each index of `parts`. A program takes and returns all parts, laid end to end along the dimension named above; each array names one. Nothing has to cross between parts.
Inputs may be any that keep to these rules, and one draw needn't show every extreme that they name: stack_deposit_tally counts, for each column, the active points from the base of the build upward. laser_target_sites holds flat cell indices; an index may repeat.
All inputs are finite; a program needn't handle non-finite values.
Results may differ from a plain program's by a relative error of at most 0.00002.
Values sent between devices are 32-bit elements; how exact they have to be, the bound alone decides.
A program may use at most 64 MiB of HBM per device.

v0:
```python
import math

import jax
import jax.numpy as jnp
from jax import lax
from jax.sharding import PartitionSpec as P

laser_energy_input = 1.5
thermal_swelling = 0.01
pressure_coef = -10.0
stiffness_coef = 300.0


def padded_2(block, sides, width):
    for axis, dim in sides:
        count = lax.axis_size(axis)
        forward = [(i, i + 1) for i in range(count - 1)]
        backward = [(target, source) for source, target in forward]
        low = lax.ppermute(
            lax.slice_in_dim(block, block.shape[dim] - width, None, axis=dim), axis, forward
        )
        high = lax.ppermute(lax.slice_in_dim(block, 0, width, axis=dim), axis, backward)
        block = jnp.concatenate([low, block, high], axis=dim)
    return block


def make_offsets():
    result = []
    for shift_one in range(-3, 4):
        for shift_two in range(-3, 4):
            for shift_three in range(-3, 4):
                radius = shift_one * shift_one + shift_two * shift_two + shift_three * shift_three
                if 0 < radius <= 9:
                    result.append((shift_one, shift_two, shift_three, math.sqrt(radius)))
    return result


def total_weight():
    running = 0.0
    for offset_item in make_offsets():
        running = running + 1.0 / offset_item[3]
    return running


def pad_side(grid_field):
    widths = [(0, 0)] * (grid_field.ndim - 1) + [(3, 3)]
    return jnp.pad(grid_field, widths)


def shifted(padded, offset_item, extent):
    return padded[
        ...,
        3 + offset_item[0] : 3 + offset_item[0] + extent[0],
        3 + offset_item[1] : 3 + offset_item[1] + extent[1],
        3 + offset_item[2] : 3 + offset_item[2] + extent[2],
    ]


def extent_of(ext_field):
    return (ext_field.shape[-3] - 6, ext_field.shape[-2] - 6, ext_field.shape[-1])


def heat_update(temp_ext, cond_ext, act_ext, laser_deposit_term):
    weight_total = total_weight()
    extent = extent_of(temp_ext)
    thermal_field_bordered = pad_side(temp_ext)
    diffusivity_bordered = pad_side(cond_ext)
    act_pad = pad_side(act_ext)
    centre_t = temp_ext[3:-3, 3:-3]
    centre_k = cond_ext[3:-3, 3:-3]
    centre_a = act_ext[3:-3, 3:-3]
    energy_flow_rate = jnp.zeros_like(centre_t)
    for offset_item in make_offsets():
        near_t = shifted(thermal_field_bordered, offset_item, extent)
        near_k = shifted(diffusivity_bordered, offset_item, extent)
        near_a = shifted(act_pad, offset_item, extent)
        energy_flow_rate = energy_flow_rate + near_a * (centre_k + near_k) * (near_t - centre_t) * (
            0.5 / (weight_total * offset_item[3])
        )
    return centre_t + centre_a * (energy_flow_rate + laser_energy_input * laser_deposit_term)


def weighted_volume(act_ext):
    extent = extent_of(act_ext)
    act_pad = pad_side(act_ext)
    centre_a = act_ext[3:-3, 3:-3]
    volume = jnp.zeros_like(centre_a)
    for offset_item in make_offsets():
        volume = volume + shifted(act_pad, offset_item, extent) * offset_item[3]
    return jnp.where(centre_a > 0, volume, 1.0)


def bond_state(disp_pad, thermal_field_bordered, offset_item, extent):
    near_u = shifted(disp_pad, offset_item, extent)
    centre_u = disp_pad[:, 3 : 3 + extent[0], 3 : 3 + extent[1], 3 : 3 + extent[2]]
    deformed = (
        offset_item[0] + near_u[0] - centre_u[0],
        offset_item[1] + near_u[1] - centre_u[1],
        offset_item[2] + near_u[2] - centre_u[2],
    )
    reach_extent = jnp.sqrt(
        deformed[0] * deformed[0] + deformed[1] * deformed[1] + deformed[2] * deformed[2]
    )
    near_t = shifted(thermal_field_bordered, offset_item, extent)
    centre_t = thermal_field_bordered[3 : 3 + extent[0], 3 : 3 + extent[1], 3 : 3 + extent[2]]
    separation = offset_item[3]
    elongation_ratio = (
        reach_extent - separation - thermal_swelling * (centre_t + near_t) * separation
    )
    return (deformed, reach_extent, elongation_ratio)


def dilatation_of(disp_ext, temp_ext, act_ext, volume):
    extent = extent_of(act_ext)
    disp_pad = pad_side(disp_ext)
    thermal_field_bordered = pad_side(temp_ext)
    act_pad = pad_side(act_ext)
    stretch_sum = jnp.zeros_like(volume)
    for offset_item in make_offsets():
        deformed, reach_extent, elongation_ratio = bond_state(
            disp_pad, thermal_field_bordered, offset_item, extent
        )
        stretch_sum = stretch_sum + shifted(act_pad, offset_item, extent) * elongation_ratio
    return act_ext[3:-3, 3:-3] * 3.0 * stretch_sum / volume


def force_density(disp_ext, temp_ext, act_ext, dilatation_ext, volume_ext):
    extent = extent_of(act_ext)
    pressure = pressure_coef * dilatation_ext / volume_ext
    stiffness = stiffness_coef / volume_ext
    disp_pad = pad_side(disp_ext)
    thermal_field_bordered = pad_side(temp_ext)
    act_pad = pad_side(act_ext)
    pressure_pad = pad_side(pressure)
    stiffness_pad = pad_side(stiffness)
    centre_p = pressure[3:-3, 3:-3]
    centre_q = stiffness[3:-3, 3:-3]
    centre_a = act_ext[3:-3, 3:-3]
    force_one = jnp.zeros_like(centre_a)
    force_two = jnp.zeros_like(centre_a)
    force_three = jnp.zeros_like(centre_a)
    for offset_item in make_offsets():
        deformed, reach_extent, elongation_ratio = bond_state(
            disp_pad, thermal_field_bordered, offset_item, extent
        )
        near_a = shifted(act_pad, offset_item, extent)
        near_p = shifted(pressure_pad, offset_item, extent)
        near_q = shifted(stiffness_pad, offset_item, extent)
        scalar = (
            near_a
            * (centre_p + near_p + (centre_q + near_q) * elongation_ratio / offset_item[3])
            / reach_extent
        )
        force_one = force_one + scalar * deformed[0]
        force_two = force_two + scalar * deformed[1]
        force_three = force_three + scalar * deformed[2]
    return centre_a[None] * jnp.stack([force_one, force_two, force_three])


def per_device(
    thermal_excess_field,
    thermal_diffusivity,
    material_shift_field,
    stack_deposit_tally,
    laser_target_sites,
):
    nodes_across_total = thermal_excess_field.shape[0]
    nodes_vertical_total = thermal_excess_field.shape[1]
    nodes_sideways_total = thermal_excess_field.shape[2]
    total_z = lax.axis_size("height") * nodes_vertical_total
    start_x = lax.axis_index(("lat", "sub")) * nodes_across_total
    start_z = lax.axis_index("height") * nodes_vertical_total

    def region_active(from_x, from_z, size_x, size_z):
        padded_top = jnp.pad(stack_deposit_tally, ((6, 6), (0, 0)))
        top_rows = lax.dynamic_slice_in_dim(padded_top, from_x + 6, size_x, 0)
        heights = from_z + jnp.arange(size_z, dtype=jnp.int32)
        return (
            (heights[None, :, None] >= 0) & (heights[None, :, None] < top_rows[:, None, :])
        ).astype(jnp.float32)

    def region_source(spot_cells, from_x, from_z, size_x, size_z):
        plane_size = total_z * nodes_sideways_total
        along_x = spot_cells // plane_size
        remainder = spot_cells % plane_size
        along_z = remainder // nodes_sideways_total
        along_y = remainder % nodes_sideways_total
        local_x = along_x - from_x
        local_z = along_z - from_z
        inside = (local_x >= 0) & (local_x < size_x) & (local_z >= 0) & (local_z < size_z)
        amounts = jnp.where(inside, 1.0, 0.0).astype(jnp.float32)
        return (
            jnp.zeros((size_x, size_z, nodes_sideways_total), jnp.float32)
            .at[jnp.clip(local_x, 0, size_x - 1), jnp.clip(local_z, 0, size_z - 1), along_y]
            .add(amounts)
        )

    rim_depth = 3
    heat_fields = padded_2(
        jnp.stack([thermal_excess_field, thermal_diffusivity]),
        ((("lat", "sub"), 1), ("height", 2)),
        3,
    )
    act_near = region_active(
        start_x - 3, start_z - 3, nodes_across_total + 6, nodes_vertical_total + 6
    )
    temp_one = heat_update(
        heat_fields[0],
        heat_fields[1],
        act_near,
        region_source(
            laser_target_sites[0], start_x, start_z, nodes_across_total, nodes_vertical_total
        ),
    )
    temp_one_ext = padded_2(temp_one, ((("lat", "sub"), 0), ("height", 1)), 3)
    temp_two = heat_update(
        temp_one_ext,
        heat_fields[1],
        act_near,
        region_source(
            laser_target_sites[1], start_x, start_z, nodes_across_total, nodes_vertical_total
        ),
    )
    mech_stack = padded_2(
        jnp.concatenate([material_shift_field, temp_two[None]], 0),
        ((("lat", "sub"), 1), ("height", 2)),
        rim_depth,
    )
    disp_ext = mech_stack[:3]
    temp_ext = mech_stack[3]
    act_big = region_active(
        start_x - 6, start_z - 6, nodes_across_total + 12, nodes_vertical_total + 12
    )
    volume_big = weighted_volume(act_big)
    dilatation_own = dilatation_of(disp_ext, temp_ext, act_big[3:-3, 3:-3], volume_big[3:-3, 3:-3])
    dilatation_ext = padded_2(dilatation_own, ((("lat", "sub"), 0), ("height", 1)), 3)
    traction_result = force_density(
        disp_ext, temp_ext, act_big[3:-3, 3:-3], dilatation_ext, volume_big
    )
    return (temp_two, traction_result)


def solution(mesh):
    return jax.shard_map(
        per_device,
        mesh=mesh,
        in_specs=(
            P(("parts", "lat", "sub"), "height", None),
            P(("parts", "lat", "sub"), "height", None),
            P(None, ("parts", "lat", "sub"), "height", None),
            P("parts", None),
            P("parts", None),
        ),
        out_specs=(
            P(("parts", "lat", "sub"), "height", None),
            P(None, ("parts", "lat", "sub"), "height", None),
        ),
        check_vma=False,
    )
```

profile of v0, /device:TPU:1, one launch (start us, length us, event | category | flops | bytes accessed | tf_op | source)
XLA Modules:
  0.0 119.4 jit_solution(14198796219333514831)
XLA Ops:
  0.6 0.8 pad_maximum_fusion.13
  1.4 4.7 %collective-permute-start = (f32[2,3,8,128]{3,2,1,0:T(8,128)S(1)}, f32[2,3,8,128]{3,2,1,0:T(8,128)S(1)}, u32[]{:S(2)}, u32[]{:S(2)}) collective-permute-start(f32[2,3,8,128]{3,2,1,0:T(8,128)S(1)} %get-tuple-element.262), channel_id=1, source_target_pairs={{0,1},{1,4},{4,5},{5,8},{8,9},{9,12},{12,13},{2,3},{3,6},{6,7},{7,... | collective-permute-start | bytes 73736 | tf_op jit(solution)/shard_map/ppermute | solution.py:19
  6.1 1.9 %collective-permute-start.1 = (f32[2,3,8,128]{3,2,1,0:T(8,128)S(1)}, f32[2,3,8,128]{3,2,1,0:T(8,128)S(1)}, u32[]{:S(2)}, u32[]{:S(2)}) collective-permute-start(f32[2,3,8,128]{3,2,1,0:T(8,128)S(1)} %get-tuple-element.263), channel_id=1, source_target_pairs={{1,0},{4,1},{5,4},{8,5},{9,8},{12,9},{13,12},{3,2},{6,3},{7,6},{10... | collective-permute-start | bytes 73736 | tf_op jit(solution)/shard_map/ppermute | solution.py:22
  9.0 2.2 %collective-permute-done.1 = f32[2,3,8,128]{3,2,1,0:T(8,128)S(1)} collective-permute-done((f32[2,3,8,128]{3,2,1,0:T(8,128)S(1)}, f32[2,3,8,128]{3,2,1,0:T(8,128)S(1)}, u32[]{:S(2)}, u32[]{:S(2)}) %collective-permute-start.1) | collective-permute-done | bytes 24608 | tf_op jit(solution)/shard_map/ppermute | solution.py:22
  11.3 3.1 %collective-permute-start.2 = (f32[2,14,3,128]{3,2,1,0:T(4,128)S(1)}, f32[2,14,3,128]{3,2,1,0:T(4,128)S(1)}, u32[]{:S(2)}, u32[]{:S(2)}) collective-permute-start(f32[2,14,3,128]{3,2,1,0:T(4,128)S(1)} %get-tuple-element.260), channel_id=1, source_target_pairs={{0,2},{1,3},{4,6},{5,7},{8,10},{9,11},{12,14},{13,15},{16,18},{17,... | collective-permute-start | bytes 129032 | tf_op jit(solution)/shard_map/ppermute | solution.py:19
  14.4 1.3 %collective-permute-start.3 = (f32[2,14,3,128]{3,2,1,0:T(4,128)S(1)}, f32[2,14,3,128]{3,2,1,0:T(4,128)S(1)}, u32[]{:S(2)}, u32[]{:S(2)}) collective-permute-start(f32[2,14,3,128]{3,2,1,0:T(4,128)S(1)} %get-tuple-element.261), channel_id=1, source_target_pairs={{2,0},{3,1},{6,4},{7,5},{10,8},{11,9},{14,12},{15,13},{18,16},{19,... | collective-permute-start | bytes 129032 | tf_op jit(solution)/shard_map/ppermute | solution.py:22
  15.8 8.2 %scatter_fusion = f32[8,8,128]{2,1,0:T(8,128)S(1)} fusion(f32[8,8,128]{2,1,0:T(8,128)S(1)} %broadcast.1351.clone, s32[128]{0:T(128)S(1)} %get-tuple-element.277, f32[128]{0:T(128)S(1)} %get-tuple-element.275), kind=kCustom, calls=%fused_computation | custom fusion | flops 128 | bytes 3072 | tf_op jit(solution)/shard_map/scatter-add | solution.py:195
  24.1 3.1 %multiply_add_fusion = f32[8,8,128]{2,1,0:T(8,128)S(1)} fusion(f32[8,8,128]{2,1,0:T(8,128)S(1)} %scatter_fusion, f32[14,14,128]{2,1,0:T(8,128)S(1)} %get-tuple-element.255, f32[14,14,128]{2,1,0:T(8,128)S(1)} %and_convert_fusion.1, f32[14,14,128]{2,1,0:T(8,128)S(1)} %get-tuple-element.254), kind=kLoop, calls=%fused_computation.4618 | loop fusion | flops 6012928 | bytes 3260416 | tf_op jit(solution)/shard_map/add | solution.py:80
  27.2 2.4 %collective-permute-start.4 = (f32[3,8,128]{2,1,0:T(8,128)S(1)}, f32[3,8,128]{2,1,0:T(8,128)S(1)}, u32[]{:S(2)}, u32[]{:S(2)}) collective-permute-start(f32[3,8,128]{2,1,0:T(8,128)S(1)} %get-tuple-element.272), channel_id=1, source_target_pairs={{0,1},{1,4},{4,5},{5,8},{8,9},{9,12},{12,13},{2,3},{3,6},{6,7},{7,... | collective-permute-start | bytes 36872 | tf_op jit(solution)/shard_map/ppermute | solution.py:19
  29.6 1.9 %collective-permute-start.5 = (f32[3,8,128]{2,1,0:T(8,128)S(1)}, f32[3,8,128]{2,1,0:T(8,128)S(1)}, u32[]{:S(2)}, u32[]{:S(2)}) collective-permute-start(f32[3,8,128]{2,1,0:T(8,128)S(1)} %get-tuple-element.273), channel_id=1, source_target_pairs={{1,0},{4,1},{5,4},{8,5},{9,8},{12,9},{13,12},{3,2},{6,3},{7,6},{10... | collective-permute-start | bytes 36872 | tf_op jit(solution)/shard_map/ppermute | solution.py:22
  31.6 3.0 %collective-permute-done.5 = f32[3,8,128]{2,1,0:T(8,128)S(1)} collective-permute-done((f32[3,8,128]{2,1,0:T(8,128)S(1)}, f32[3,8,128]{2,1,0:T(8,128)S(1)}, u32[]{:S(2)}, u32[]{:S(2)}) %collective-permute-start.5) | collective-permute-done | bytes 12320 | tf_op jit(solution)/shard_map/ppermute | solution.py:22
  34.6 4.3 %collective-permute-start.6 = (f32[14,3,128]{2,1,0:T(4,128)S(1)}, f32[14,3,128]{2,1,0:T(4,128)S(1)}, u32[]{:S(2)}, u32[]{:S(2)}) collective-permute-start(f32[14,3,128]{2,1,0:T(4,128)S(1)} %get-tuple-element.268), channel_id=1, source_target_pairs={{0,2},{1,3},{4,6},{5,7},{8,10},{9,11},{12,14},{13,15},{16,18},{17,... | collective-permute-start | bytes 64520 | tf_op jit(solution)/shard_map/ppermute | solution.py:19
  38.9 1.3 %collective-permute-start.7 = (f32[14,3,128]{2,1,0:T(4,128)S(1)}, f32[14,3,128]{2,1,0:T(4,128)S(1)}, u32[]{:S(2)}, u32[]{:S(2)}) collective-permute-start(f32[14,3,128]{2,1,0:T(4,128)S(1)} %get-tuple-element.269), channel_id=1, source_target_pairs={{2,0},{3,1},{6,4},{7,5},{10,8},{11,9},{14,12},{15,13},{18,16},{19,... | collective-permute-start | bytes 64520 | tf_op jit(solution)/shard_map/ppermute | solution.py:22
  40.3 8.2 %scatter_fusion.1 = f32[8,8,128]{2,1,0:T(8,128)S(1)} fusion(f32[8,8,128]{2,1,0:T(8,128)S(1)} %broadcast.1351.clone.1, s32[128]{0:T(128)S(1)} %get-tuple-element.276, f32[128]{0:T(128)S(1)} %get-tuple-element.274), kind=kCustom, calls=%fused_computation.1 | custom fusion | flops 128 | bytes 3072 | tf_op jit(solution)/shard_map/scatter-add | solution.py:195
  48.8 3.1 %fusion.234 = f32[8,8,128]{2,1,0:T(8,128)S(1)} fusion(f32[8,8,128]{2,1,0:T(8,128)S(1)} %multiply_add_fusion, f32[3,8,128]{2,1,0:T(8,128)S(1)} %collective-permute-done.5, f32[14,14,134]{2,1,0:T(8,128)S(1)} %select_maximum_fusion.5, f32[14,11,128]{2,1,0:T(8,128)S(1)} %get-tuple-element.267, f32[14,11,128]{2,1,0:T(8,128)S(1)} %get-tuple-element.266, ...), kind=kLoop, calls=%fused_computation.1056 | loop fusion | flops 6062080 | bytes 6053888 | tf_op jit(solution)/shard_map/add | solution.py:80
  52.0 2.2 %collective-permute-start.8 = (f32[4,3,8,128]{3,2,1,0:T(8,128)S(1)}, f32[4,3,8,128]{3,2,1,0:T(8,128)S(1)}, u32[]{:S(2)}, u32[]{:S(2)}) collective-permute-start(f32[4,3,8,128]{3,2,1,0:T(8,128)S(1)} %get-tuple-element.258), channel_id=1, source_target_pairs={{0,1},{1,4},{4,5},{5,8},{8,9},{9,12},{12,13},{2,3},{3,6},{6,7},{7,... | collective-permute-start | bytes 147464 | tf_op jit(solution)/shard_map/ppermute | solution.py:19
  54.2 2.1 %collective-permute-start.9 = (f32[4,3,8,128]{3,2,1,0:T(8,128)S(1)}, f32[4,3,8,128]{3,2,1,0:T(8,128)S(1)}, u32[]{:S(2)}, u32[]{:S(2)}) collective-permute-start(f32[4,3,8,128]{3,2,1,0:T(8,128)S(1)} %get-tuple-element.259), channel_id=1, source_target_pairs={{1,0},{4,1},{5,4},{8,5},{9,8},{12,9},{13,12},{3,2},{6,3},{7,6},{10... | collective-permute-start | bytes 147464 | tf_op jit(solution)/shard_map/ppermute | solution.py:22
  56.3 3.0 %broadcast_divide_fusion = (f32[14,14,128]{2,1,0:T(8,128)S(1)}, f32[14,14,128]{2,1,0:T(8,128)S(1)}) fusion(f32[20,20,128]{2,1,0:T(8,128)S(1)} %and_convert_fusion), kind=kLoop, calls=%fused_computation.1029 | loop fusion | flops 5996032 | bytes 3772416 | tf_op jit(solution)/shard_map/div | solution.py:130
  59.7 4.3 %collective-permute-start.10 = (f32[4,14,3,128]{3,2,1,0:T(4,128)S(1)}, f32[4,14,3,128]{3,2,1,0:T(4,128)S(1)}, u32[]{:S(2)}, u32[]{:S(2)}) collective-permute-start(f32[4,14,3,128]{3,2,1,0:T(4,128)S(1)} %get-tuple-element.252), channel_id=1, source_target_pairs={{0,2},{1,3},{4,6},{5,7},{8,10},{9,11},{12,14},{13,15},{16,18},{17,... | collective-permute-start | bytes 258056 | tf_op jit(solution)/shard_map/ppermute | solution.py:19
  63.9 1.3 %collective-permute-start.11 = (f32[4,14,3,128]{3,2,1,0:T(4,128)S(1)}, f32[4,14,3,128]{3,2,1,0:T(4,128)S(1)}, u32[]{:S(2)}, u32[]{:S(2)}) collective-permute-start(f32[4,14,3,128]{3,2,1,0:T(4,128)S(1)} %get-tuple-element.253), channel_id=1, source_target_pairs={{2,0},{3,1},{6,4},{7,5},{10,8},{11,9},{14,12},{15,13},{18,16},{19,... | collective-permute-start | bytes 258056 | tf_op jit(solution)/shard_map/ppermute | solution.py:22
  65.4 0.8 collective-permute-done.10
  66.2 4.1 %collective-permute-done.11 = f32[4,14,3,128]{3,2,1,0:T(4,128)S(1)} collective-permute-done((f32[4,14,3,128]{3,2,1,0:T(4,128)S(1)}, f32[4,14,3,128]{3,2,1,0:T(4,128)S(1)}, u32[]{:S(2)}, u32[]{:S(2)}) %collective-permute-start.11) | collective-permute-done | bytes 86048 | tf_op jit(solution)/shard_map/ppermute | solution.py:22
  72.7 8.4 %slice_divide_fusion = (f32[8,8,128]{2,1,0:T(8,128)S(1)}, f32[8,8,128]{2,1,0:T(8,128)}, f32[8,8,128]{2,1,0:T(8,128)}, f32[8,8,128]{2,1,0:T(8,128)}, f32[8,8,128]...) fusion(f32[14,14,128]{2,1,0:T(8,128)S(1)} %get-tuple-element.18, ...), kind=kLoop, calls=%fused_computation.2837 | loop fusion | flops 14123008 | bytes 15532032 | tf_op jit(solution)/shard_map/div | solution.py:124
  81.1 4.2 %collective-permute-start.12 = (f32[3,8,128]{2,1,0:T(8,128)S(1)}, f32[3,8,128]{2,1,0:T(8,128)S(1)}, u32[]{:S(2)}, u32[]{:S(2)}) collective-permute-start(f32[3,8,128]{2,1,0:T(8,128)S(1)} %get-tuple-element.270), channel_id=1, source_target_pairs={{0,1},{1,4},{4,5},{5,8},{8,9},{9,12},{12,13},{2,3},{3,6},{6,7},{7,... | collective-permute-start | bytes 36872 | tf_op jit(solution)/shard_map/ppermute | solution.py:19
  85.3 1.9 %collective-permute-start.13 = (f32[3,8,128]{2,1,0:T(8,128)S(1)}, f32[3,8,128]{2,1,0:T(8,128)S(1)}, u32[]{:S(2)}, u32[]{:S(2)}) collective-permute-start(f32[3,8,128]{2,1,0:T(8,128)S(1)} %get-tuple-element.271), channel_id=1, source_target_pairs={{1,0},{4,1},{5,4},{8,5},{9,8},{12,9},{13,12},{3,2},{6,3},{7,6},{10... | collective-permute-start | bytes 36872 | tf_op jit(solution)/shard_map/ppermute | solution.py:22
  87.3 3.1 %collective-permute-done.13 = f32[3,8,128]{2,1,0:T(8,128)S(1)} collective-permute-done((f32[3,8,128]{2,1,0:T(8,128)S(1)}, f32[3,8,128]{2,1,0:T(8,128)S(1)}, u32[]{:S(2)}, u32[]{:S(2)}) %collective-permute-start.13) | collective-permute-done | bytes 12320 | tf_op jit(solution)/shard_map/ppermute | solution.py:22
  90.4 1.3 %collective-permute-start.14 = (f32[14,3,128]{2,1,0:T(4,128)S(1)}, f32[14,3,128]{2,1,0:T(4,128)S(1)}, u32[]{:S(2)}, u32[]{:S(2)}) collective-permute-start(f32[14,3,128]{2,1,0:T(4,128)S(1)} %get-tuple-element.264), channel_id=1, source_target_pairs={{0,2},{1,3},{4,6},{5,7},{8,10},{9,11},{12,14},{13,15},{16,18},{17,... | collective-permute-start | bytes 64520 | tf_op jit(solution)/shard_map/ppermute | solution.py:19
  91.7 1.5 %collective-permute-start.15 = (f32[14,3,128]{2,1,0:T(4,128)S(1)}, f32[14,3,128]{2,1,0:T(4,128)S(1)}, u32[]{:S(2)}, u32[]{:S(2)}) collective-permute-start(f32[14,3,128]{2,1,0:T(4,128)S(1)} %get-tuple-element.265), channel_id=1, source_target_pairs={{2,0},{3,1},{6,4},{7,5},{10,8},{11,9},{14,12},{15,13},{18,16},{19,... | collective-permute-start | bytes 64520 | tf_op jit(solution)/shard_map/ppermute | solution.py:22
  93.2 3.1 %collective-permute-done.15 = f32[14,3,128]{2,1,0:T(4,128)S(1)} collective-permute-done((f32[14,3,128]{2,1,0:T(4,128)S(1)}, f32[14,3,128]{2,1,0:T(4,128)S(1)}, u32[]{:S(2)}, u32[]{:S(2)}) %collective-permute-start.15) | collective-permute-done | bytes 21536 | tf_op jit(solution)/shard_map/ppermute | solution.py:22
  110.7 6.0 %add_bitcast_fusion.2 = (f32[1,8,8,128]{3,2,1,0:T(8,128)S(1)}, f32[8,8,128]{2,1,0:T(8,128)S(1)}, f32[8,8,128]{2,1,0:T(8,128)S(1)}, f32[8,8,128]{2,1,0:T(8,128)S(...) fusion(f32[8,8,128]{2,1,0:T(8,128)S(1)} %get-tuple-element.221,, ...), kind=kLoop, calls=%fused_computation.4495 | loop fusion | flops 11460608 | bytes 15106048 | tf_op jit(solution)/shard_map/stack | solution.py:157
  116.7 1.0 add_bitcast_fusion.1
  117.7 1.0 add_bitcast_fusion
  (237 shorter events, 18.8 us)
Async XLA Ops:
  1.4 7.4 %copy-start.80 = (s32[64,128]{1,0:T(8,128)S(1)}, s32[64,128]{1,0:T(8,128)}, u32[]{:S(2)}) copy-start(s32[64,128]{1,0:T(8,128)} %param.8) | copy-start | bytes 98308
  1.4 7.6 %collective-permute-start = (f32[2,3,8,128]{3,2,1,0:T(8,128)S(1)}, f32[2,3,8,128]{3,2,1,0:T(8,128)S(1)}, u32[]{:S(2)}, u32[]{:S(2)}) collective-permute-start(f32[2,3,8,128]{3,2,1,0:T(8,128)S(1)} %get-tuple-element.262), channel_id=1, source_target_pairs={{0,1},{1,4},{4,5},{5,8},{8,9},{9,12},{12,13},{2,3},{3,6},{6,7},{7,... | collective-permute-start | bytes 73736 | tf_op jit(solution)/shard_map/ppermute | solution.py:19
  6.1 5.1 %collective-permute-start.1 = (f32[2,3,8,128]{3,2,1,0:T(8,128)S(1)}, f32[2,3,8,128]{3,2,1,0:T(8,128)S(1)}, u32[]{:S(2)}, u32[]{:S(2)}) collective-permute-start(f32[2,3,8,128]{3,2,1,0:T(8,128)S(1)} %get-tuple-element.263), channel_id=1, source_target_pairs={{1,0},{4,1},{5,4},{8,5},{9,8},{12,9},{13,12},{3,2},{6,3},{7,6},{10... | collective-permute-start | bytes 73736 | tf_op jit(solution)/shard_map/ppermute | solution.py:22
  8.9 2.4 %copy-start.8 = (f32[8,8,128]{2,1,0:T(8,128)S(1)}, f32[8,8,128]{2,1,0:T(8,128)}, u32[]{:S(2)}) copy-start(f32[8,8,128]{2,1,0:T(8,128)} %param.5) | copy-start | bytes 98308
  9.0 2.3 %copy-start.7 = (f32[8,8,128]{2,1,0:T(8,128)S(1)}, f32[8,8,128]{2,1,0:T(8,128)}, u32[]{:S(2)}) copy-start(f32[8,8,128]{2,1,0:T(8,128)} %param.6) | copy-start | bytes 98308
  11.3 12.7 %collective-permute-start.2 = (f32[2,14,3,128]{3,2,1,0:T(4,128)S(1)}, f32[2,14,3,128]{3,2,1,0:T(4,128)S(1)}, u32[]{:S(2)}, u32[]{:S(2)}) collective-permute-start(f32[2,14,3,128]{3,2,1,0:T(4,128)S(1)} %get-tuple-element.260), channel_id=1, source_target_pairs={{0,2},{1,3},{4,6},{5,7},{8,10},{9,11},{12,14},{13,15},{16,18},{17,... | collective-permute-start | bytes 129032 | tf_op jit(solution)/shard_map/ppermute | solution.py:19
  14.4 9.6 %collective-permute-start.3 = (f32[2,14,3,128]{3,2,1,0:T(4,128)S(1)}, f32[2,14,3,128]{3,2,1,0:T(4,128)S(1)}, u32[]{:S(2)}, u32[]{:S(2)}) collective-permute-start(f32[2,14,3,128]{3,2,1,0:T(4,128)S(1)} %get-tuple-element.261), channel_id=1, source_target_pairs={{2,0},{3,1},{6,4},{7,5},{10,8},{11,9},{14,12},{15,13},{18,16},{19,... | collective-permute-start | bytes 129032 | tf_op jit(solution)/shard_map/ppermute | solution.py:22
  27.2 4.4 %collective-permute-start.4 = (f32[3,8,128]{2,1,0:T(8,128)S(1)}, f32[3,8,128]{2,1,0:T(8,128)S(1)}, u32[]{:S(2)}, u32[]{:S(2)}) collective-permute-start(f32[3,8,128]{2,1,0:T(8,128)S(1)} %get-tuple-element.272), channel_id=1, source_target_pairs={{0,1},{1,4},{4,5},{5,8},{8,9},{9,12},{12,13},{2,3},{3,6},{6,7},{7,... | collective-permute-start | bytes 36872 | tf_op jit(solution)/shard_map/ppermute | solution.py:19
  29.6 5.0 %collective-permute-start.5 = (f32[3,8,128]{2,1,0:T(8,128)S(1)}, f32[3,8,128]{2,1,0:T(8,128)S(1)}, u32[]{:S(2)}, u32[]{:S(2)}) collective-permute-start(f32[3,8,128]{2,1,0:T(8,128)S(1)} %get-tuple-element.273), channel_id=1, source_target_pairs={{1,0},{4,1},{5,4},{8,5},{9,8},{12,9},{13,12},{3,2},{6,3},{7,6},{10... | collective-permute-start | bytes 36872 | tf_op jit(solution)/shard_map/ppermute | solution.py:22
  34.6 13.9 %collective-permute-start.6 = (f32[14,3,128]{2,1,0:T(4,128)S(1)}, f32[14,3,128]{2,1,0:T(4,128)S(1)}, u32[]{:S(2)}, u32[]{:S(2)}) collective-permute-start(f32[14,3,128]{2,1,0:T(4,128)S(1)} %get-tuple-element.268), channel_id=1, source_target_pairs={{0,2},{1,3},{4,6},{5,7},{8,10},{9,11},{12,14},{13,15},{16,18},{17,... | collective-permute-start | bytes 64520 | tf_op jit(solution)/shard_map/ppermute | solution.py:19
  38.9 9.7 %collective-permute-start.7 = (f32[14,3,128]{2,1,0:T(4,128)S(1)}, f32[14,3,128]{2,1,0:T(4,128)S(1)}, u32[]{:S(2)}, u32[]{:S(2)}) collective-permute-start(f32[14,3,128]{2,1,0:T(4,128)S(1)} %get-tuple-element.269), channel_id=1, source_target_pairs={{2,0},{3,1},{6,4},{7,5},{10,8},{11,9},{14,12},{15,13},{18,16},{19,... | collective-permute-start | bytes 64520 | tf_op jit(solution)/shard_map/ppermute | solution.py:22
  48.8 3.1 %copy-start = (f32[3,8,8,128]{3,2,1,0:T(8,128)S(1)}, f32[3,8,8,128]{3,2,1,0:T(8,128)}, u32[]{:S(2)}) copy-start(f32[3,8,8,128]{3,2,1,0:T(8,128)} %param.7) | copy-start | bytes 294916
  51.9 20.7 %copy-start.1 = (f32[8,8,128]{2,1,0:T(8,128)}, f32[8,8,128]{2,1,0:T(8,128)S(1)}, u32[]{:S(2)}) copy-start(f32[8,8,128]{2,1,0:T(8,128)S(1)} %fusion.234) | copy-start | bytes 98308
  52.0 7.3 %collective-permute-start.8 = (f32[4,3,8,128]{3,2,1,0:T(8,128)S(1)}, f32[4,3,8,128]{3,2,1,0:T(8,128)S(1)}, u32[]{:S(2)}, u32[]{:S(2)}) collective-permute-start(f32[4,3,8,128]{3,2,1,0:T(8,128)S(1)} %get-tuple-element.258), channel_id=1, source_target_pairs={{0,1},{1,4},{4,5},{5,8},{8,9},{9,12},{12,13},{2,3},{3,6},{6,7},{7,... | collective-permute-start | bytes 147464 | tf_op jit(solution)/shard_map/ppermute | solution.py:19
  54.2 5.4 %collective-permute-start.9 = (f32[4,3,8,128]{3,2,1,0:T(8,128)S(1)}, f32[4,3,8,128]{3,2,1,0:T(8,128)S(1)}, u32[]{:S(2)}, u32[]{:S(2)}) collective-permute-start(f32[4,3,8,128]{3,2,1,0:T(8,128)S(1)} %get-tuple-element.259), channel_id=1, source_target_pairs={{1,0},{4,1},{5,4},{8,5},{9,8},{12,9},{13,12},{3,2},{6,3},{7,6},{10... | collective-permute-start | bytes 147464 | tf_op jit(solution)/shard_map/ppermute | solution.py:22
  59.7 6.5 %collective-permute-start.10 = (f32[4,14,3,128]{3,2,1,0:T(4,128)S(1)}, f32[4,14,3,128]{3,2,1,0:T(4,128)S(1)}, u32[]{:S(2)}, u32[]{:S(2)}) collective-permute-start(f32[4,14,3,128]{3,2,1,0:T(4,128)S(1)} %get-tuple-element.252), channel_id=1, source_target_pairs={{0,2},{1,3},{4,6},{5,7},{8,10},{9,11},{12,14},{13,15},{16,18},{17,... | collective-permute-start | bytes 258056 | tf_op jit(solution)/shard_map/ppermute | solution.py:19
  63.9 6.3 %collective-permute-start.11 = (f32[4,14,3,128]{3,2,1,0:T(4,128)S(1)}, f32[4,14,3,128]{3,2,1,0:T(4,128)S(1)}, u32[]{:S(2)}, u32[]{:S(2)}) collective-permute-start(f32[4,14,3,128]{3,2,1,0:T(4,128)S(1)} %get-tuple-element.253), channel_id=1, source_target_pairs={{2,0},{3,1},{6,4},{7,5},{10,8},{11,9},{14,12},{15,13},{18,16},{19,... | collective-permute-start | bytes 258056 | tf_op jit(solution)/shard_map/ppermute | solution.py:22
  81.1 6.2 %collective-permute-start.12 = (f32[3,8,128]{2,1,0:T(8,128)S(1)}, f32[3,8,128]{2,1,0:T(8,128)S(1)}, u32[]{:S(2)}, u32[]{:S(2)}) collective-permute-start(f32[3,8,128]{2,1,0:T(8,128)S(1)} %get-tuple-element.270), channel_id=1, source_target_pairs={{0,1},{1,4},{4,5},{5,8},{8,9},{9,12},{12,13},{2,3},{3,6},{6,7},{7,... | collective-permute-start | bytes 36872 | tf_op jit(solution)/shard_map/ppermute | solution.py:19
  85.3 5.0 %collective-permute-start.13 = (f32[3,8,128]{2,1,0:T(8,128)S(1)}, f32[3,8,128]{2,1,0:T(8,128)S(1)}, u32[]{:S(2)}, u32[]{:S(2)}) collective-permute-start(f32[3,8,128]{2,1,0:T(8,128)S(1)} %get-tuple-element.271), channel_id=1, source_target_pairs={{1,0},{4,1},{5,4},{8,5},{9,8},{12,9},{13,12},{3,2},{6,3},{7,6},{10... | collective-permute-start | bytes 36872 | tf_op jit(solution)/shard_map/ppermute | solution.py:22
  90.4 2.8 %collective-permute-start.14 = (f32[14,3,128]{2,1,0:T(4,128)S(1)}, f32[14,3,128]{2,1,0:T(4,128)S(1)}, u32[]{:S(2)}, u32[]{:S(2)}) collective-permute-start(f32[14,3,128]{2,1,0:T(4,128)S(1)} %get-tuple-element.264), channel_id=1, source_target_pairs={{0,2},{1,3},{4,6},{5,7},{8,10},{9,11},{12,14},{13,15},{16,18},{17,... | collective-permute-start | bytes 64520 | tf_op jit(solution)/shard_map/ppermute | solution.py:19
  91.7 4.6 %collective-permute-start.15 = (f32[14,3,128]{2,1,0:T(4,128)S(1)}, f32[14,3,128]{2,1,0:T(4,128)S(1)}, u32[]{:S(2)}, u32[]{:S(2)}) collective-permute-start(f32[14,3,128]{2,1,0:T(4,128)S(1)} %get-tuple-element.265), channel_id=1, source_target_pairs={{2,0},{3,1},{6,4},{7,5},{10,8},{11,9},{14,12},{15,13},{18,16},{19,... | collective-permute-start | bytes 64520 | tf_op jit(solution)/shard_map/ppermute | solution.py:22
  93.2 3.2 %copy-start.78 = (f32[8,8,128]{2,1,0:T(8,128)S(1)}, f32[8,8,128]{2,1,0:T(8,128)}, u32[]{:S(2)}) copy-start(f32[8,8,128]{2,1,0:T(8,128)} %get-tuple-element.142) | copy-start | bytes 98308
  93.2 3.2 %copy-start.79 = (f32[8,8,128]{2,1,0:T(8,128)S(1)}, f32[8,8,128]{2,1,0:T(8,128)}, u32[]{:S(2)}) copy-start(f32[8,8,128]{2,1,0:T(8,128)} %get-tuple-element.143) | copy-start | bytes 98308
  108.7 1.2 copy-start.32
  108.8 1.2 copy-start.33
  108.8 1.2 copy-start.34
  108.8 1.2 copy-start.35
  108.8 1.2 copy-start.36
  108.8 1.2 copy-start.37
  108.8 1.2 copy-start.38
  108.8 1.2 copy-start.39
  108.8 1.2 copy-start.40
  (66 other events, 55.3 us)
where the time goes:
time: 122 us; the launch traced here: 119 us
  other arithmetic  49 us (40%)
  starting transfers between devices  39.7 us (33%)
  waiting for transfers between devices  16.6 us (14%)
  local copies, waits for them, and re-layouts  12.2 us (10%)
  between operations  1.82 us (1%)
    ppermute x8, starting transfers between devices, padded_2(): lax.ppermute(lax.slice_in_dim(block, block.shape[dim] - width, None, axis...  26.5 us
    scatter-add x2, other arithmetic, region_source(): return jnp.zeros((size_x, size_z, nodes_sideways_total), jnp.float32).at[...  16.5 us
    ppermute x8, waiting for transfers between devices, padded_2(): lax.ppermute(lax.slice_in_dim(block, 0, width, axis=dim), axis, backward)  15.8 us
    ppermute x8, starting transfers between devices, padded_2(): lax.ppermute(lax.slice_in_dim(block, 0, width, axis=dim), axis, backward)  13.2 us
    unnamed x164, local copies, waits for them, and re-layouts  12 us
    div x1, other arithmetic, dilatation_of(): return act_ext[3:-3, 3:-3] * 3.0 * stretch_sum / volume  8.4 us
    another operation x3, other arithmetic, force_density(): return centre_a[None] * jnp.stack([force_one, force_two, force_three])  8.04 us
    add x2, other arithmetic, heat_update(): centre_t + centre_a * (energy_flow_rate + laser_energy_input * laser_depo...  6.17 us
  transfers between devices with their start and end apart: 16, of which 7 were waited for; matrix products, arithmetic and copies ran while one was open for 17% of the time, Pallas kernels for 0%

commit v1 on v0

v1 whole, which is shorter than its diff:
```python
import functools
import math

import jax
import jax.numpy as jnp
from jax import lax
from jax.experimental import pallas as pl
from jax.experimental.pallas import tpu as pltpu
from jax.sharding import PartitionSpec as P

laser_energy_input = 1.5
thermal_swelling = 0.01
pressure_coef = -10.0
stiffness_coef = 300.0

RIM = 3
REACH = RIM * RIM
BASE = 8

OFFSETS = [
    (a, b, c)
    for c in range(-RIM, RIM + 1)
    for a in range(-RIM, RIM + 1)
    for b in range(-RIM, RIM + 1)
    if 0 < a * a + b * b + c * c <= REACH
]
PLANE = [
    (a, b)
    for a in range(-RIM, RIM + 1)
    for b in range(-RIM, RIM + 1)
    if a * a + b * b <= REACH
]
SQUARES = sorted({a * a + b * b for a, b in PLANE})
TOTAL_WEIGHT = sum(1.0 / math.sqrt(a * a + b * b + c * c) for a, b, c in OFFSETS)
DIRECTIONS = [(dx, dz) for dx in (-1, 0, 1) for dz in (-1, 0, 1) if (dx, dz) != (0, 0)]
PHASE_FIELDS = (5, 2, 1, 1)


def inverse_distance(square):
    return 1.0 / math.sqrt(square)


def kernel(
    temp_in,
    cond_in,
    shift_in,
    tally_in,
    sites_in,
    temp_out,
    force_out,
    e1,
    e2,
    e3,
    e4,
    p1,
    p2,
    p3,
    p4,
    z1,
    z2,
    z3,
    z4,
    c1,
    c2,
    c3,
    c4,
    tally,
    sites,
    act,
    act_k,
    act_t,
    act_kt,
    source,
    sum_a,
    sum_ak,
    vol,
    dil,
    lean,
    total,
    normal,
    strain,
    local_sem,
    send_sem,
    recv_sem,
):
    nx, nz, lanes = temp_in.shape
    across_total = tally_in.shape[0]
    n_sub = lax.axis_size("sub")
    n_lateral = lax.axis_size("lat") * n_sub
    n_height = lax.axis_size("height")
    total_z = n_height * nz
    at_x = lax.axis_index("lat") * n_sub + lax.axis_index("sub")
    at_z = lax.axis_index("height")
    start_x = at_x * nx
    start_z = at_z * nz
    own_x = slice(RIM, RIM + nx)
    own_z = slice(BASE, BASE + nz)
    ext, packed, faces, corners = (e1, e2, e3, e4), (p1, p2, p3, p4), (z1, z2, z3, z4), (c1, c2, c3, c4)

    def exists(dx, dz):
        result = None
        for step, at, count in ((dx, at_x, n_lateral), (dz, at_z, n_height)):
            if step:
                test = at + step >= 0 if step < 0 else at + step < count
                result = test if result is None else jnp.logical_and(result, test)
        return result

    def device(dx, dz):
        to_x = at_x + dx
        return {"lat": to_x // n_sub, "sub": to_x % n_sub, "height": at_z + dz}

    def message(phase, which):
        dx, dz = DIRECTIONS[which]
        if dz == 0:
            here = slice(RIM, 2 * RIM) if dx < 0 else slice(nx, RIM + nx)
            there = slice(RIM + nx, 2 * RIM + nx) if dx < 0 else slice(0, RIM)
            src = ext[phase].at[:, here, own_z]
            dst = ext[phase].at[:, there, own_z]
        else:
            side, far = (0, 1) if dz < 0 else (1, 0)
            if dx == 0:
                src, dst = packed[phase].at[side], faces[phase].at[far]
            else:
                rows = slice(0, 16) if dx < 0 else slice(RIM * nx - 16, RIM * nx)
                src = packed[phase].at[side, :, rows]
                dst = corners[phase].at[far, 1 if dx < 0 else 0]
        return pltpu.make_async_remote_copy(
            src_ref=src,
            dst_ref=dst,
            send_sem=send_sem.at[phase, which],
            recv_sem=recv_sem.at[phase, which],
            device_id=device(dx, dz),
            device_id_type=pl.DeviceIdType.MESH,
        )

    def pack(phase):
        for f in range(PHASE_FIELDS[phase]):
            for x in range(nx):
                tile = ext[phase][f, RIM + x, own_z, :]
                packed[phase][0, f, RIM * x : RIM * x + RIM, :] = tile[0:RIM]
                packed[phase][1, f, RIM * x : RIM * x + RIM, :] = tile[nz - RIM : nz]

    def send(phase):
        for which, (dx, dz) in enumerate(DIRECTIONS):

            @pl.when(exists(dx, dz))
            def _(which=which):
                message(phase, which).start()

    def receive(phase):
        for which, (dx, dz) in enumerate(DIRECTIONS):

            @pl.when(exists(-dx, -dz))
            def _(which=which):
                message(phase, which).wait_recv()

        for f in range(PHASE_FIELDS[phase]):
            for side in range(2):
                rows = slice(BASE - RIM, BASE) if side == 0 else slice(BASE + nz, BASE + nz + RIM)
                for x in range(nx):
                    ext[phase][f, RIM + x, rows, :] = faces[phase][side, f, RIM * x : RIM * x + RIM, :]
                for i in range(RIM):
                    low = 16 - REACH + RIM * i
                    ext[phase][f, i, rows, :] = corners[phase][side, 0, f, low : low + RIM, :]
                    ext[phase][f, RIM + nx + i, rows, :] = corners[phase][
                        side, 1, f, RIM * i : RIM * i + RIM, :
                    ]

    loads = [
        pltpu.make_async_copy(temp_in, e1.at[0, own_x, own_z], local_sem.at[0]),
        pltpu.make_async_copy(cond_in, e1.at[1, own_x, own_z], local_sem.at[1]),
        pltpu.make_async_copy(shift_in, e1.at[2:5, own_x, own_z], local_sem.at[2]),
        pltpu.make_async_copy(tally_in, tally, local_sem.at[3]),
        pltpu.make_async_copy(sites_in, sites, local_sem.at[4]),
    ]
    for load in loads:
        load.start()

    for phase in range(4):
        for f in range(PHASE_FIELDS[phase]):
            zeros = jnp.zeros((RIM, nz, lanes), jnp.float32)
            ext[phase][f, 0:RIM, own_z, :] = zeros
            ext[phase][f, RIM + nx : 2 * RIM + nx, own_z, :] = zeros
        faces[phase][...] = jnp.zeros_like(faces[phase])
        corners[phase][...] = jnp.zeros_like(corners[phase])

    barrier = pltpu.get_barrier_semaphore()
    for dx, dz in DIRECTIONS:

        @pl.when(exists(dx, dz))
        def _(dx=dx, dz=dz):
            pl.semaphore_signal(
                barrier, inc=1, device_id=device(dx, dz), device_id_type=pl.DeviceIdType.MESH
            )

    for load in loads[:3]:
        load.wait()
    pack(0)
    beside = jnp.where(at_x > 0, 1, 0) + jnp.where(at_x + 1 < n_lateral, 1, 0)
    stacked = jnp.where(at_z > 0, 1, 0) + jnp.where(at_z + 1 < n_height, 1, 0)
    pl.semaphore_wait(barrier, (beside + 1) * (stacked + 1) - 1)

    send(0)

    lane = lax.broadcasted_iota(jnp.int32, (nz, lanes), 1)

    def frame(value, c):
        return value if c == 0 else pltpu.roll(value, c % lanes, 1)

    def unframe(value, c):
        if c == 0:
            return value
        inside = lane < lanes - c if c > 0 else lane >= -c
        return jnp.where(inside, pltpu.roll(value, (-c) % lanes, 1), 0.0)

    def near(ref, x, a, b):
        return ref[x + (RIM + a), BASE + b : BASE + b + nz, :]

    def ring_sums(ref, x):
        sums = {}
        for a, b in PLANE:
            square = a * a + b * b
            value = near(ref, x, a, b)
            sums[square] = sums[square] + value if square in sums else value
        return sums

    def weighted(sums, weight):
        result = None
        for c in range(RIM + 1):
            part = None
            for square in SQUARES:
                if 0 < square + c * c <= REACH:
                    term = sums[square] * weight(square + c * c)
                    part = term if part is None else part + term
            for sign in (1, -1) if c else (1,):
                moved = unframe(part, sign * c)
                result = moved if result is None else result + moved
        return result

    for load in loads[3:]:
        load.wait()
    heights = start_z - BASE + lax.broadcasted_iota(jnp.int32, (act.shape[1], lanes), 0)
    for x in range(nx + 2 * RIM):
        line = start_x + (x - RIM)
        count = tally[pl.ds(jnp.clip(line, 0, across_total - 1), 1), :]
        count = jnp.where(jnp.logical_and(line >= 0, line < across_total), count, 0)
        act[x] = jnp.where((heights >= 0) & (heights < count), 1.0, 0.0)

    for step in range(2):
        spots = sites[step : step + 1, :]
        n_spots = spots.shape[1]
        rows = []
        for x in range(nx):
            level = start_z + lax.broadcasted_iota(jnp.int32, (nz, n_spots), 0)
            gap = spots - ((start_x + x) * total_z + level) * lanes
            rows.append(jnp.where((gap >= 0) & (gap < lanes), 1.0, 0.0))
        row_hit = jnp.concatenate(rows, 0)
        lane_hit = jnp.where(
            lax.broadcasted_iota(jnp.int32, (lanes, n_spots), 0) == lax.rem(spots, lanes), 1.0, 0.0
        )
        hits = lax.dot_general(
            row_hit, lane_hit, (((1,), (1,)), ((), ())), preferred_element_type=jnp.float32
        )
        source[step] = hits.reshape(nx, nz, lanes)

    @pl.loop(0, nx)
    def _(x):
        sums = ring_sums(act, x)
        sum_a[x] = weighted(sums, inverse_distance)
        mass = weighted(sums, math.sqrt)
        mass = jnp.where(near(act, x, 0, 0) > 0, mass, 1.0)
        vol[x] = mass
        e2[1, x + RIM, own_z, :] = stiffness_coef / mass

    receive(0)

    def heat(field, step, x):
        rate_t = weighted(ring_sums(act_t, x), inverse_distance)
        rate_kt = weighted(ring_sums(act_kt, x), inverse_distance)
        temp = near(field, x, 0, 0)
        cond = near(e1.at[1], x, 0, 0)
        flow = cond * rate_t + rate_kt - temp * (cond * sum_a[x] + sum_ak[x])
        return temp + near(act, x, 0, 0) * (
            flow * (0.5 / TOTAL_WEIGHT) + laser_energy_input * source[step, x]
        )

    @pl.loop(0, nx + 2 * RIM)
    def _(x):
        act_k[x] = act[x] * e1[1, x]
        act_t[x] = act[x] * e1[0, x]
        act_kt[x] = act_k[x] * e1[0, x]

    @pl.loop(0, nx)
    def _(x):
        sum_ak[x] = weighted(ring_sums(act_k, x), inverse_distance)
        e2[0, x + RIM, own_z, :] = heat(e1.at[0], 0, x)

    pack(1)
    send(1)

    def geometry(x):
        centre = [near(e1.at[2 + k], x, 0, 0) for k in range(3)]
        stretched = None
        leaning = [None] * 3
        bond = 0
        for c in range(-RIM, RIM + 1):
            moved = [frame(value, c) for value in centre]
            first = {a: moved[0] - float(a) for a in range(-RIM, RIM + 1)}
            second = {b: moved[1] - float(b) for b in range(-RIM, RIM + 1)}
            third = moved[2] - float(c)
            part = None
            parts = [None] * 3
            for a, b, other in OFFSETS:
                if other != c:
                    continue
                separation = math.sqrt(a * a + b * b + c * c)
                d = (
                    near(e1.at[2], x, a, b) - first[a],
                    near(e1.at[3], x, a, b) - second[b],
                    near(e1.at[4], x, a, b) - third,
                )
                square = d[0] * d[0] + d[1] * d[1] + d[2] * d[2]
                inverse = lax.rsqrt(square)
                there = near(act, x, a, b)
                change = square * inverse - separation
                strain[x, bond] = change * (1.0 / separation)
                masked = inverse * there
                change = change * there
                part = change if part is None else part + change
                for k in range(3):
                    unit = d[k] * masked
                    normal[x, bond, k] = unit
                    parts[k] = unit if parts[k] is None else parts[k] + unit
                bond += 1
            part = unframe(part, c)
            stretched = part if stretched is None else stretched + part
            for k in range(3):
                leaned = unframe(parts[k], c)
                leaning[k] = leaned if leaning[k] is None else leaning[k] + leaned
        dil[x] = stretched
        for k in range(3):
            lean[k, x] = leaning[k]

    @pl.loop(0, nx)
    def _(x):
        geometry(x)

    receive(1)

    @pl.loop(0, nx + 2 * RIM)
    def _(x):
        act_t[x] = act[x] * e2[0, x]
        act_kt[x] = act_k[x] * e2[0, x]

    @pl.loop(0, nx)
    def _(x):
        e3[0, x + RIM, own_z, :] = heat(e2.at[0], 1, x)

    pack(2)
    send(2)
    store_temp = pltpu.make_async_copy(e3.at[0, own_x, own_z], temp_out, local_sem.at[0])
    store_temp.start()

    receive(2)

    @pl.loop(0, nx + 2 * RIM)
    def _(x):
        act_t[x] = act[x] * e3[0, x]

    @pl.loop(0, nx)
    def _(x):
        mass = vol[x]
        swell = weighted(ring_sums(act_t, x), math.sqrt) + near(e3.at[0], x, 0, 0) * mass
        change = near(act, x, 0, 0) * 3.0 * (dil[x] - thermal_swelling * swell) / mass
        e4[0, x + RIM, own_z, :] = pressure_coef * change / mass

    pack(3)
    send(3)

    @pl.loop(0, nx)
    def _(x):
        result = [None] * 3
        bond = 0
        for c in range(-RIM, RIM + 1):
            stiff = frame(near(e2.at[1], x, 0, 0), c)
            warm = frame(near(e3.at[0], x, 0, 0), c)
            parts = [None] * 3
            for a, b, other in OFFSETS:
                if other != c:
                    continue
                swell = (warm + near(e3.at[0], x, a, b)) * thermal_swelling
                scale = (stiff + near(e2.at[1], x, a, b)) * (strain[x, bond] - swell)
                for k in range(3):
                    term = normal[x, bond, k] * scale
                    parts[k] = term if parts[k] is None else parts[k] + term
                bond += 1
            for k in range(3):
                moved = unframe(parts[k], c)
                result[k] = moved if result[k] is None else result[k] + moved
        for k in range(3):
            total[k, x] = result[k]

    receive(3)

    @pl.loop(0, nx)
    def _(x):
        pressure = near(e4.at[0], x, 0, 0)
        result = [total[k, x] + pressure * lean[k, x] for k in range(3)]
        bond = 0
        for c in range(-RIM, RIM + 1):
            parts = [None] * 3
            for a, b, other in OFFSETS:
                if other != c:
                    continue
                push = near(e4.at[0], x, a, b)
                for k in range(3):
                    term = normal[x, bond, k] * push
                    parts[k] = term if parts[k] is None else parts[k] + term
                bond += 1
            for k in range(3):
                result[k] = result[k] + unframe(parts[k], c)
        for k in range(3):
            force_out[k, x] = near(act, x, 0, 0) * result[k]

    store_temp.wait()
    for phase in range(4):
        for which, (dx, dz) in enumerate(DIRECTIONS):

            @pl.when(exists(dx, dz))
            def _(phase=phase, which=which):
                message(phase, which).wait_send()


def per_device(temp, cond, shift, tally, sites):
    nx, nz, lanes = temp.shape
    wide = nx + 2 * RIM
    tall = 2 * BASE + nz
    f32 = jnp.float32
    bonds = len(OFFSETS)
    scratch = (
        [pltpu.VMEM((n, wide, tall, lanes), f32) for n in PHASE_FIELDS]
        + [pltpu.VMEM((2, n, RIM * nx, lanes), f32) for n in PHASE_FIELDS]
        + [pltpu.VMEM((2, n, RIM * nx, lanes), f32) for n in PHASE_FIELDS]
        + [pltpu.VMEM((2, 2, n, 16, lanes), f32) for n in PHASE_FIELDS]
        + [pltpu.VMEM(tally.shape, jnp.int32), pltpu.VMEM(sites.shape, jnp.int32)]
        + [pltpu.VMEM((wide, tall, lanes), f32)] * 4
        + [pltpu.VMEM((2, nx, nz, lanes), f32)]
        + [pltpu.VMEM((nx, nz, lanes), f32)] * 4
        + [pltpu.VMEM((3, nx, nz, lanes), f32)] * 2
        + [pltpu.VMEM((nx, bonds, 3, nz, lanes), f32), pltpu.VMEM((nx, bonds, nz, lanes), f32)]
        + [
            pltpu.SemaphoreType.DMA((5,)),
            pltpu.SemaphoreType.DMA((4, len(DIRECTIONS))),
            pltpu.SemaphoreType.DMA((4, len(DIRECTIONS))),
        ]
    )
    return pl.pallas_call(
        kernel,
        out_shape=(
            jax.ShapeDtypeStruct(temp.shape, f32),
            jax.ShapeDtypeStruct(shift.shape, f32),
        ),
        in_specs=[pl.BlockSpec(memory_space=pl.ANY)] * 5,
        out_specs=(
            pl.BlockSpec(memory_space=pl.ANY),
            pl.BlockSpec(memory_space=pltpu.VMEM),
        ),
        scratch_shapes=scratch,
        compiler_params=pltpu.CompilerParams(
            collective_id=0, has_side_effects=True, vmem_limit_bytes=40 * 2**20
        ),
    )(temp, cond, shift, tally, sites)


def solution(mesh):
    return jax.shard_map(
        per_device,
        mesh=mesh,
        in_specs=(
            P(("parts", "lat", "sub"), "height", None),
            P(("parts", "lat", "sub"), "height", None),
            P(None, ("parts", "lat", "sub"), "height", None),
            P("parts", None),
            P("parts", None),
        ),
        out_specs=(
            P(("parts", "lat", "sub"), "height", None),
            P(None, ("parts", "lat", "sub"), "height", None),
        ),
        check_vma=False,
    )
```

time: 122 us -> 28.4 us (0.23); the launches traced: 119 us -> 28 us
  other arithmetic: 49 us -> 0 us
  starting transfers between devices: 39.7 us -> 0 us
  Pallas kernels: 0 us -> 22.3 us
  waiting for transfers between devices: 16.6 us -> 0 us
  local copies, waits for them, and re-layouts: 12.2 us -> 5.09 us
    ppermute x16 -> x0, starting transfers between devices: 39.7 us -> none  [the longest x8 26.5 us: padded_2(): lax.ppermute(lax.slice_in_dim(block, block.shape[dim] - width, None, axis...]
    pallas_call x0 -> x1, Pallas kernels: none -> 22.3 us  [per_device(): pl.pallas_call(kernel, out_shape=(jax.ShapeDtypeStruct(temp.shape, f32),...]
    ppermute x16 -> x0, waiting for transfers between devices: 16.6 us -> none  [the longest x8 15.8 us: padded_2(): lax.ppermute(lax.slice_in_dim(block, 0, width, axis=dim), axis, backward)]
    scatter-add x2 -> x0, other arithmetic: 16.5 us -> none  [region_source(): return jnp.zeros((size_x, size_z, nodes_sideways_total), jnp.float32).at[...]
    div x21 -> x0, other arithmetic: 13.9 us -> none  [the longest x1 8.4 us: dilatation_of(): return act_ext[3:-3, 3:-3] * 3.0 * stretch_sum / volume]
    another operation x3 -> x0, other arithmetic: 8.04 us -> none  [force_density(): return centre_a[None] * jnp.stack([force_one, force_two, force_three])]
    unnamed x164 -> x12, local copies, waits for them, and re-layouts: 12 us -> 5.09 us
    add x4 -> x0, other arithmetic: 6.18 us -> none  [the longest x2 6.17 us: heat_update(): centre_t + centre_a * (energy_flow_rate + laser_energy_input * laser_depo...]
  transfers between devices with their start and end apart: 16 -> 0, of which waited for: 7 -> 0; matrix products, arithmetic and copies ran while one was open for 17% -> 0% of each run, Pallas kernels for 0% -> 0%
where the time goes in v1:
time: 28.4 us; the launch traced here: 28 us
  Pallas kernels  22.3 us (79%)
  local copies, waits for them, and re-layouts  5.09 us (18%)
  between operations  0.65 us (2%)
    pallas_call x1, Pallas kernels, per_device(): pl.pallas_call(kernel, out_shape=(jax.ShapeDtypeStruct(temp.shape, f32),...  22.3 us
    unnamed x12, local copies, waits for them, and re-layouts  5.09 us

profile of v1, /device:TPU:1, one launch (start us, length us, event | category | flops | bytes accessed | tf_op | source)
XLA Modules:
  0.0 28.0 jit_solution(6891082333276402773)
XLA Ops:
  0.6 0.0 copy-start
  0.6 0.9 %copy-done = f32[3,8,8,128]{3,2,1,0:T(8,128)S(1)} copy-done((f32[3,8,8,128]{3,2,1,0:T(8,128)S(1)}, f32[3,8,8,128]{3,2,1,0:T(8,128)}, u32[]{:S(2)}) %copy-start) | copy-done | bytes 98328
  1.5 0.0 copy-start.1
  1.5 0.8 %copy-done.1 = f32[8,8,128]{2,1,0:T(8,128)S(1)} copy-done((f32[8,8,128]{2,1,0:T(8,128)S(1)}, f32[8,8,128]{2,1,0:T(8,128)}, u32[]{:S(2)}) %copy-start.1) | copy-done | bytes 32792
  2.3 0.0 copy-start.2
  2.3 0.8 %copy-done.2 = f32[8,8,128]{2,1,0:T(8,128)S(1)} copy-done((f32[8,8,128]{2,1,0:T(8,128)S(1)}, f32[8,8,128]{2,1,0:T(8,128)}, u32[]{:S(2)}) %copy-start.2) | copy-done | bytes 32792
  3.0 0.0 copy-start.3
  3.0 0.8 %copy-done.3 = s32[64,128]{1,0:T(8,128)S(1)} copy-done((s32[64,128]{1,0:T(8,128)S(1)}, s32[64,128]{1,0:T(8,128)}, u32[]{:S(2)}) %copy-start.3) | copy-done | bytes 32792
  3.8 0.0 copy-start.4
  3.8 0.7 %copy-done.4 = s32[2,128]{1,0:T(2,128)S(1)} copy-done((s32[2,128]{1,0:T(2,128)S(1)}, s32[2,128]{1,0:T(2,128)}, u32[]{:S(2)}) %copy-start.4) | copy-done | bytes 1048
  4.5 22.3 %shard_map.68 = (f32[8,8,128]{2,1,0:T(8,128)S(1)}, f32[3,8,8,128]{3,2,1,0:T(8,128)S(1)}) custom-call(f32[8,8,128]{2,1,0:T(8,128)S(1)} %copy-done.1, f32[8,8,128]{2,1,0:T(8,128)S(1)} %copy-done.2, f32[3,8,8,128]{3,2,1,0:T(8,128)S(1)} %copy-done, s32[64,128]{1,0:T(8,128)S(1)} %copy-done.3, s32[2,128]{1,0:T(2,128)S(1)} %copy-done.4), custom_call_target="tpu_custom_call" | custom-call | tf_op jit(solution)/shard_map/pallas_call | solution.py:457
  26.8 0.6 %copy.9 = f32[8,8,128]{2,1,0:T(8,128)} copy(f32[8,8,128]{2,1,0:T(8,128)S(1)} %get-tuple-element.4) | data formatting | bytes 65536
  27.4 0.6 %copy.10 = f32[3,8,8,128]{3,2,1,0:T(8,128)} copy(f32[3,8,8,128]{3,2,1,0:T(8,128)S(1)} %get-tuple-element.5) | data formatting | bytes 196608
Async XLA Ops:
  0.6 0.9 %copy-start = (f32[3,8,8,128]{3,2,1,0:T(8,128)S(1)}, f32[3,8,8,128]{3,2,1,0:T(8,128)}, u32[]{:S(2)}) copy-start(f32[3,8,8,128]{3,2,1,0:T(8,128)} %shift_in.1) | copy-start | bytes 294916
  1.5 0.8 %copy-start.1 = (f32[8,8,128]{2,1,0:T(8,128)S(1)}, f32[8,8,128]{2,1,0:T(8,128)}, u32[]{:S(2)}) copy-start(f32[8,8,128]{2,1,0:T(8,128)} %temp_in.1) | copy-start | bytes 98308
  2.3 0.8 %copy-start.2 = (f32[8,8,128]{2,1,0:T(8,128)S(1)}, f32[8,8,128]{2,1,0:T(8,128)}, u32[]{:S(2)}) copy-start(f32[8,8,128]{2,1,0:T(8,128)} %cond_in.1) | copy-start | bytes 98308
  3.0 0.8 %copy-start.3 = (s32[64,128]{1,0:T(8,128)S(1)}, s32[64,128]{1,0:T(8,128)}, u32[]{:S(2)}) copy-start(s32[64,128]{1,0:T(8,128)} %tally_in.1) | copy-start | bytes 98308
  3.8 0.7 %copy-start.4 = (s32[2,128]{1,0:T(2,128)S(1)}, s32[2,128]{1,0:T(2,128)}, u32[]{:S(2)}) copy-start(s32[2,128]{1,0:T(2,128)} %sites_in.1) | copy-start | bytes 3076

commit v2 on v1

--- a/solution.py
+++ b/solution.py
@@ -33,7 +33,8 @@
 SQUARES = sorted({a * a + b * b for a, b in PLANE})
 TOTAL_WEIGHT = sum(1.0 / math.sqrt(a * a + b * b + c * c) for a, b, c in OFFSETS)
 DIRECTIONS = [(dx, dz) for dx in (-1, 0, 1) for dz in (-1, 0, 1) if (dx, dz) != (0, 0)]
-PHASE_FIELDS = (5, 2, 1, 1)
+PHASE_FIELDS = (2, 3, 2, 1, 1)
+VMEM_BYTES = 63 * 2**20
 
 
 def inverse_distance(square):
@@ -48,18 +49,22 @@
     sites_in,
     temp_out,
     force_out,
+    e0,
     e1,
     e2,
     e3,
     e4,
+    p0,
     p1,
     p2,
     p3,
     p4,
+    z0,
     z1,
     z2,
     z3,
     z4,
+    c0,
     c1,
     c2,
     c3,
@@ -70,12 +75,12 @@
     act_k,
     act_t,
     act_kt,
+    warmth,
     source,
     sum_a,
     sum_ak,
     vol,
     dil,
-    lean,
     total,
     normal,
     strain,
@@ -95,7 +100,9 @@
     start_z = at_z * nz
     own_x = slice(RIM, RIM + nx)
     own_z = slice(BASE, BASE + nz)
-    ext, packed, faces, corners = (e1, e2, e3, e4), (p1, p2, p3, p4), (z1, z2, z3, z4), (c1, c2, c3, c4)
+    ext, packed = (e0, e1, e2, e3, e4), (p0, p1, p2, p3, p4)
+    faces, corners = (z0, z1, z2, z3, z4), (c0, c1, c2, c3, c4)
+    phases = len(PHASE_FIELDS)
 
     def exists(dx, dz):
         result = None
@@ -167,16 +174,16 @@
                     ]
 
     loads = [
-        pltpu.make_async_copy(temp_in, e1.at[0, own_x, own_z], local_sem.at[0]),
-        pltpu.make_async_copy(cond_in, e1.at[1, own_x, own_z], local_sem.at[1]),
-        pltpu.make_async_copy(shift_in, e1.at[2:5, own_x, own_z], local_sem.at[2]),
+        pltpu.make_async_copy(temp_in, e0.at[0, own_x, own_z], local_sem.at[0]),
+        pltpu.make_async_copy(cond_in, e0.at[1, own_x, own_z], local_sem.at[1]),
+        pltpu.make_async_copy(shift_in, e1.at[:, own_x, own_z], local_sem.at[2]),
         pltpu.make_async_copy(tally_in, tally, local_sem.at[3]),
         pltpu.make_async_copy(sites_in, sites, local_sem.at[4]),
     ]
     for load in loads:
         load.start()
 
-    for phase in range(4):
+    for phase in range(phases):
         for f in range(PHASE_FIELDS[phase]):
             zeros = jnp.zeros((RIM, nz, lanes), jnp.float32)
             ext[phase][f, 0:RIM, own_z, :] = zeros
@@ -193,7 +200,7 @@
                 barrier, inc=1, device_id=device(dx, dz), device_id_type=pl.DeviceIdType.MESH
             )
 
-    for load in loads[:3]:
+    for load in loads[:2]:
         load.wait()
     pack(0)
     beside = jnp.where(at_x > 0, 1, 0) + jnp.where(at_x + 1 < n_lateral, 1, 0)
@@ -201,6 +208,9 @@
     pl.semaphore_wait(barrier, (beside + 1) * (stacked + 1) - 1)
 
     send(0)
+    loads[2].wait()
+    pack(1)
+    send(1)
 
     lane = lax.broadcasted_iota(jnp.int32, (nz, lanes), 1)
 
@@ -278,7 +288,7 @@
         rate_t = weighted(ring_sums(act_t, x), inverse_distance)
         rate_kt = weighted(ring_sums(act_kt, x), inverse_distance)
         temp = near(field, x, 0, 0)
-        cond = near(e1.at[1], x, 0, 0)
+        cond = near(e0.at[1], x, 0, 0)
         flow = cond * rate_t + rate_kt - temp * (cond * sum_a[x] + sum_ak[x])
         return temp + near(act, x, 0, 0) * (
             flow * (0.5 / TOTAL_WEIGHT) + laser_energy_input * source[step, x]
@@ -286,22 +296,21 @@
 
     @pl.loop(0, nx + 2 * RIM)
     def _(x):
-        act_k[x] = act[x] * e1[1, x]
-        act_t[x] = act[x] * e1[0, x]
-        act_kt[x] = act_k[x] * e1[0, x]
+        act_k[x] = act[x] * e0[1, x]
+        act_t[x] = act[x] * e0[0, x]
+        act_kt[x] = act_k[x] * e0[0, x]
 
     @pl.loop(0, nx)
     def _(x):
         sum_ak[x] = weighted(ring_sums(act_k, x), inverse_distance)
-        e2[0, x + RIM, own_z, :] = heat(e1.at[0], 0, x)
-
-    pack(1)
-    send(1)
+        e2[0, x + RIM, own_z, :] = heat(e0.at[0], 0, x)
+
+    pack(2)
+    send(2)
 
     def geometry(x):
-        centre = [near(e1.at[2 + k], x, 0, 0) for k in range(3)]
+        centre = [near(e1.at[k], x, 0, 0) for k in range(3)]
         stretched = None
-        leaning = [None] * 3
         bond = 0
         for c in range(-RIM, RIM + 1):
             moved = [frame(value, c) for value in centre]
@@ -309,15 +318,14 @@
             second = {b: moved[1] - float(b) for b in range(-RIM, RIM + 1)}
             third = moved[2] - float(c)
             part = None
-            parts = [None] * 3
             for a, b, other in OFFSETS:
                 if other != c:
                     continue
                 separation = math.sqrt(a * a + b * b + c * c)
                 d = (
-                    near(e1.at[2], x, a, b) - first[a],
-                    near(e1.at[3], x, a, b) - second[b],
-                    near(e1.at[4], x, a, b) - third,
+                    near(e1.at[0], x, a, b) - first[a],
+                    near(e1.at[1], x, a, b) - second[b],
+                    near(e1.at[2], x, a, b) - third,
                 )
                 square = d[0] * d[0] + d[1] * d[1] + d[2] * d[2]
                 inverse = lax.rsqrt(square)
@@ -328,24 +336,20 @@
                 change = change * there
                 part = change if part is None else part + change
                 for k in range(3):
-                    unit = d[k] * masked
-                    normal[x, bond, k] = unit
-                    parts[k] = unit if parts[k] is None else parts[k] + unit
+                    normal[x, bond, k] = d[k] * masked
                 bond += 1
             part = unframe(part, c)
             stretched = part if stretched is None else stretched + part
-            for k in range(3):
-                leaned = unframe(parts[k], c)
-                leaning[k] = leaned if leaning[k] is None else leaning[k] + leaned
         dil[x] = stretched
-        for k in range(3):
-            lean[k, x] = leaning[k]
-
-    @pl.loop(0, nx)
+
+    half = nx // 2
+    receive(1)
+
+    @pl.loop(0, half)
     def _(x):
         geometry(x)
 
-    receive(1)
+    receive(2)
 
     @pl.loop(0, nx + 2 * RIM)
     def _(x):
@@ -354,18 +358,23 @@
 
     @pl.loop(0, nx)
     def _(x):
-        e3[0, x + RIM, own_z, :] = heat(e2.at[0], 1, x)
-
-    pack(2)
-    send(2)
-    store_temp = pltpu.make_async_copy(e3.at[0, own_x, own_z], temp_out, local_sem.at[0])
-    store_temp.start()
-
-    receive(2)
+        warmed = heat(e2.at[0], 1, x)
+        e3[0, x + RIM, own_z, :] = warmed
+        temp_out[x] = warmed
+
+    pack(3)
+    send(3)
+
+    @pl.loop(half, nx)
+    def _(x):
+        geometry(x)
+
+    receive(3)
 
     @pl.loop(0, nx + 2 * RIM)
     def _(x):
         act_t[x] = act[x] * e3[0, x]
+        warmth[x] = thermal_swelling * e3[0, x]
 
     @pl.loop(0, nx)
     def _(x):
@@ -374,8 +383,8 @@
         change = near(act, x, 0, 0) * 3.0 * (dil[x] - thermal_swelling * swell) / mass
         e4[0, x + RIM, own_z, :] = pressure_coef * change / mass
 
-    pack(3)
-    send(3)
+    pack(4)
+    send(4)
 
     @pl.loop(0, nx)
     def _(x):
@@ -383,12 +392,12 @@
         bond = 0
         for c in range(-RIM, RIM + 1):
             stiff = frame(near(e2.at[1], x, 0, 0), c)
-            warm = frame(near(e3.at[0], x, 0, 0), c)
+            warm = frame(near(warmth, x, 0, 0), c)
             parts = [None] * 3
             for a, b, other in OFFSETS:
                 if other != c:
                     continue
-                swell = (warm + near(e3.at[0], x, a, b)) * thermal_swelling
+                swell = warm + near(warmth, x, a, b)
                 scale = (stiff + near(e2.at[1], x, a, b)) * (strain[x, bond] - swell)
                 for k in range(3):
                     term = normal[x, bond, k] * scale
@@ -400,19 +409,20 @@
         for k in range(3):
             total[k, x] = result[k]
 
-    receive(3)
+    receive(4)
 
     @pl.loop(0, nx)
     def _(x):
         pressure = near(e4.at[0], x, 0, 0)
-        result = [total[k, x] + pressure * lean[k, x] for k in range(3)]
+        result = [total[k, x] for k in range(3)]
         bond = 0
         for c in range(-RIM, RIM + 1):
+            own = frame(pressure, c)
             parts = [None] * 3
             for a, b, other in OFFSETS:
                 if other != c:
                     continue
-                push = near(e4.at[0], x, a, b)
+                push = own + near(e4.at[0], x, a, b)
                 for k in range(3):
                     term = normal[x, bond, k] * push
                     parts[k] = term if parts[k] is None else parts[k] + term
@@ -422,13 +432,23 @@
         for k in range(3):
             force_out[k, x] = near(act, x, 0, 0) * result[k]
 
-    store_temp.wait()
-    for phase in range(4):
+    for phase in range(phases):
         for which, (dx, dz) in enumerate(DIRECTIONS):
 
             @pl.when(exists(dx, dz))
             def _(phase=phase, which=which):
                 message(phase, which).wait_send()
+
+
+def hand_over(temp, force, temp_out, force_out, sem):
+    copies = [
+        pltpu.make_async_copy(temp, temp_out, sem.at[0]),
+        pltpu.make_async_copy(force, force_out, sem.at[1]),
+    ]
+    for copy in copies:
+        copy.start()
+    for copy in copies:
+        copy.wait()
 
 
 def per_device(temp, cond, shift, tally, sites):
@@ -443,33 +463,38 @@
         + [pltpu.VMEM((2, n, RIM * nx, lanes), f32) for n in PHASE_FIELDS]
         + [pltpu.VMEM((2, 2, n, 16, lanes), f32) for n in PHASE_FIELDS]
         + [pltpu.VMEM(tally.shape, jnp.int32), pltpu.VMEM(sites.shape, jnp.int32)]
-        + [pltpu.VMEM((wide, tall, lanes), f32)] * 4
+        + [pltpu.VMEM((wide, tall, lanes), f32)] * 5
         + [pltpu.VMEM((2, nx, nz, lanes), f32)]
         + [pltpu.VMEM((nx, nz, lanes), f32)] * 4
-        + [pltpu.VMEM((3, nx, nz, lanes), f32)] * 2
+        + [pltpu.VMEM((3, nx, nz, lanes), f32)]
         + [pltpu.VMEM((nx, bonds, 3, nz, lanes), f32), pltpu.VMEM((nx, bonds, nz, lanes), f32)]
         + [
             pltpu.SemaphoreType.DMA((5,)),
-            pltpu.SemaphoreType.DMA((4, len(DIRECTIONS))),
-            pltpu.SemaphoreType.DMA((4, len(DIRECTIONS))),
+            pltpu.SemaphoreType.DMA((len(PHASE_FIELDS), len(DIRECTIONS))),
+            pltpu.SemaphoreType.DMA((len(PHASE_FIELDS), len(DIRECTIONS))),
         ]
     )
+    whole = pl.BlockSpec(memory_space=pltpu.VMEM)
+    results = pl.pallas_call(
+        kernel,
+        out_shape=(pltpu.VMEM(temp.shape, f32), pltpu.VMEM(shift.shape, f32)),
+        in_specs=[pl.BlockSpec(memory_space=pl.ANY)] * 5,
+        out_specs=(whole, whole),
+        scratch_shapes=scratch,
+        compiler_params=pltpu.CompilerParams(
+            collective_id=0, has_side_effects=True, vmem_limit_bytes=VMEM_BYTES
+        ),
+    )(temp, cond, shift, tally, sites)
     return pl.pallas_call(
-        kernel,
+        hand_over,
         out_shape=(
             jax.ShapeDtypeStruct(temp.shape, f32),
             jax.ShapeDtypeStruct(shift.shape, f32),
         ),
-        in_specs=[pl.BlockSpec(memory_space=pl.ANY)] * 5,
-        out_specs=(
-            pl.BlockSpec(memory_space=pl.ANY),
-            pl.BlockSpec(memory_space=pltpu.VMEM),
-        ),
-        scratch_shapes=scratch,
-        compiler_params=pltpu.CompilerParams(
-            collective_id=0, has_side_effects=True, vmem_limit_bytes=40 * 2**20
-        ),
-    )(temp, cond, shift, tally, sites)
+        in_specs=[pl.BlockSpec(memory_space=pl.ANY)] * 2,
+        out_specs=(pl.BlockSpec(memory_space=pl.ANY),) * 2,
+        scratch_shapes=[pltpu.SemaphoreType.DMA((2,))],
+    )(*results)
 
 
 def solution(mesh):

time: 28.4 us -> 28.2 us (level)
  Pallas kernels: 22.3 us -> 26.2 us
  local copies, waits for them, and re-layouts: 5.09 us -> 1.22 us
    pallas_call x1 -> x2, Pallas kernels: 22.3 us -> 26.2 us  [the longest x1 21.1 us: per_device(): pl.pallas_call(kernel, out_shape=(pltpu.VMEM(temp.shape, f32), pltpu.VMEM...]
    unnamed x12 -> x4, local copies, waits for them, and re-layouts: 5.09 us -> 1.22 us
where the time goes in v2:
time: 28.2 us; the launch traced here: 28 us
  Pallas kernels  26.2 us (93%)
  local copies, waits for them, and re-layouts  1.22 us (4%)
  between operations  0.65 us (2%)
    pallas_call x1, Pallas kernels, per_device(): pl.pallas_call(kernel, out_shape=(pltpu.VMEM(temp.shape, f32), pltpu.VMEM...  21.1 us
    pallas_call x1, Pallas kernels, per_device(): pl.pallas_call(hand_over, out_shape=(jax.ShapeDtypeStruct(temp.shape, f32...  5.09 us
    unnamed x4, local copies, waits for them, and re-layouts  1.22 us

profile of v2, /device:TPU:1, one launch (start us, length us, event | category | flops | bytes accessed | tf_op | source)
XLA Modules:
  0.0 28.0 jit_solution(17740138105407398329)
XLA Ops:
  0.6 21.1 %shard_map.68 = (f32[8,8,128]{2,1,0:T(8,128)S(1)}, f32[3,8,8,128]{3,2,1,0:T(8,128)S(1)}) custom-call(f32[8,8,128]{2,1,0:T(8,128)} %temp_in.1, f32[8,8,128]{2,1,0:T(8,128)} %cond_in.1, f32[3,8,8,128]{3,2,1,0:T(8,128)} %shift_in.1, s32[64,128]{1,0:T(8,128)} %tally_in.1, s32[2,128]{1,0:T(2,128)} %sites_in.1), custom_call_target="tpu_custom_call" | custom-call | tf_op jit(solution)/shard_map/pallas_call | solution.py:478
  21.7 0.0 copy-start
  21.7 0.6 %copy-done = f32[3,8,8,128]{3,2,1,0:T(8,128)} copy-done((f32[3,8,8,128]{3,2,1,0:T(8,128)}, f32[3,8,8,128]{3,2,1,0:T(8,128)S(1)}, u32[]{:S(2)}) %copy-start) | copy-done | bytes 98328
  22.4 0.0 copy-start.1
  22.4 0.6 %copy-done.1 = f32[8,8,128]{2,1,0:T(8,128)} copy-done((f32[8,8,128]{2,1,0:T(8,128)}, f32[8,8,128]{2,1,0:T(8,128)S(1)}, u32[]{:S(2)}) %copy-start.1) | copy-done | bytes 32792
  23.0 5.1 %shard_map.69 = (f32[8,8,128]{2,1,0:T(8,128)}, f32[3,8,8,128]{3,2,1,0:T(8,128)}) custom-call(f32[8,8,128]{2,1,0:T(8,128)} %copy-done.1, f32[3,8,8,128]{3,2,1,0:T(8,128)} %copy-done), custom_call_target="tpu_custom_call" | custom-call | tf_op jit(solution)/shard_map/pallas_call | solution.py:488
Async XLA Ops:
  21.7 0.6 %copy-start = (f32[3,8,8,128]{3,2,1,0:T(8,128)}, f32[3,8,8,128]{3,2,1,0:T(8,128)S(1)}, u32[]{:S(2)}) copy-start(f32[3,8,8,128]{3,2,1,0:T(8,128)S(1)} %get-tuple-element.5.force) | copy-start | bytes 294916
  22.4 0.6 %copy-start.1 = (f32[8,8,128]{2,1,0:T(8,128)}, f32[8,8,128]{2,1,0:T(8,128)S(1)}, u32[]{:S(2)}) copy-start(f32[8,8,128]{2,1,0:T(8,128)S(1)} %get-tuple-element.4.temp) | copy-start | bytes 98308

commit v3 on v2

--- a/solution.py
+++ b/solution.py
@@ -440,17 +440,6 @@
                 message(phase, which).wait_send()
 
 
-def hand_over(temp, force, temp_out, force_out, sem):
-    copies = [
-        pltpu.make_async_copy(temp, temp_out, sem.at[0]),
-        pltpu.make_async_copy(force, force_out, sem.at[1]),
-    ]
-    for copy in copies:
-        copy.start()
-    for copy in copies:
-        copy.wait()
-
-
 def per_device(temp, cond, shift, tally, sites):
     nx, nz, lanes = temp.shape
     wide = nx + 2 * RIM
@@ -475,7 +464,7 @@
         ]
     )
     whole = pl.BlockSpec(memory_space=pltpu.VMEM)
-    results = pl.pallas_call(
+    return pl.pallas_call(
         kernel,
         out_shape=(pltpu.VMEM(temp.shape, f32), pltpu.VMEM(shift.shape, f32)),
         in_specs=[pl.BlockSpec(memory_space=pl.ANY)] * 5,
@@ -485,16 +474,6 @@
             collective_id=0, has_side_effects=True, vmem_limit_bytes=VMEM_BYTES
         ),
     )(temp, cond, shift, tally, sites)
-    return pl.pallas_call(
-        hand_over,
-        out_shape=(
-            jax.ShapeDtypeStruct(temp.shape, f32),
-            jax.ShapeDtypeStruct(shift.shape, f32),
-        ),
-        in_specs=[pl.BlockSpec(memory_space=pl.ANY)] * 2,
-        out_specs=(pl.BlockSpec(memory_space=pl.ANY),) * 2,
-        scratch_shapes=[pltpu.SemaphoreType.DMA((2,))],
-    )(*results)
 
 
 def solution(mesh):

time: 28.2 us -> 23.1 us (0.82)
  Pallas kernels: 26.2 us -> 21.1 us
    pallas_call x1 -> x0, Pallas kernels: 5.09 us -> none  [per_device(): pl.pallas_call(hand_over, out_shape=(jax.ShapeDtypeStruct(temp.shape, f32...]
    unnamed x4 -> x2, local copies, waits for them, and re-layouts: 1.22 us -> 1.26 us
where the time goes in v3:
time: 23.1 us; the launch traced here: 23 us
  Pallas kernels  21.1 us (91%)
  local copies, waits for them, and re-layouts  1.26 us (5%)
  between operations  0.64 us (3%)
    pallas_call x1, Pallas kernels, per_device(): pl.pallas_call(kernel, out_shape=(pltpu.VMEM(temp.shape, f32), pltpu.VMEM...  21.1 us
    unnamed x2, local copies, waits for them, and re-layouts  1.26 us

profile of v3, /device:TPU:1, one launch (start us, length us, event | category | flops | bytes accessed | tf_op | source)
XLA Modules:
  0.0 23.0 jit_solution(9113010979711070348)
XLA Ops:
  0.6 21.1 %shard_map.68 = (f32[8,8,128]{2,1,0:T(8,128)S(1)}, f32[3,8,8,128]{3,2,1,0:T(8,128)S(1)}) custom-call(f32[8,8,128]{2,1,0:T(8,128)} %temp_in.1, f32[8,8,128]{2,1,0:T(8,128)} %cond_in.1, f32[3,8,8,128]{3,2,1,0:T(8,128)} %shift_in.1, s32[64,128]{1,0:T(8,128)} %tally_in.1, s32[2,128]{1,0:T(2,128)} %sites_in.1), custom_call_target="tpu_custom_call" | custom-call | tf_op jit(solution)/shard_map/pallas_call | solution.py:467
  21.7 0.6 %copy.9 = f32[8,8,128]{2,1,0:T(8,128)} copy(f32[8,8,128]{2,1,0:T(8,128)S(1)} %get-tuple-element.2) | data formatting | bytes 65536
  22.3 0.6 %copy.10 = f32[3,8,8,128]{3,2,1,0:T(8,128)} copy(f32[3,8,8,128]{3,2,1,0:T(8,128)S(1)} %get-tuple-element.3) | data formatting | bytes 196608

commit v4 on v3

--- a/solution.py
+++ b/solution.py
@@ -273,7 +273,7 @@
         )
         source[step] = hits.reshape(nx, nz, lanes)
 
-    @pl.loop(0, nx)
+    @pl.loop(0, nx, unroll=2)
     def _(x):
         sums = ring_sums(act, x)
         sum_a[x] = weighted(sums, inverse_distance)
@@ -294,13 +294,13 @@
             flow * (0.5 / TOTAL_WEIGHT) + laser_energy_input * source[step, x]
         )
 
-    @pl.loop(0, nx + 2 * RIM)
+    @pl.loop(0, nx + 2 * RIM, unroll=2)
     def _(x):
         act_k[x] = act[x] * e0[1, x]
         act_t[x] = act[x] * e0[0, x]
         act_kt[x] = act_k[x] * e0[0, x]
 
-    @pl.loop(0, nx)
+    @pl.loop(0, nx, unroll=2)
     def _(x):
         sum_ak[x] = weighted(ring_sums(act_k, x), inverse_distance)
         e2[0, x + RIM, own_z, :] = heat(e0.at[0], 0, x)
@@ -351,12 +351,12 @@
 
     receive(2)
 
-    @pl.loop(0, nx + 2 * RIM)
+    @pl.loop(0, nx + 2 * RIM, unroll=2)
     def _(x):
         act_t[x] = act[x] * e2[0, x]
         act_kt[x] = act_k[x] * e2[0, x]
 
-    @pl.loop(0, nx)
+    @pl.loop(0, nx, unroll=2)
     def _(x):
         warmed = heat(e2.at[0], 1, x)
         e3[0, x + RIM, own_z, :] = warmed
@@ -371,12 +371,12 @@
 
     receive(3)
 
-    @pl.loop(0, nx + 2 * RIM)
+    @pl.loop(0, nx + 2 * RIM, unroll=2)
     def _(x):
         act_t[x] = act[x] * e3[0, x]
         warmth[x] = thermal_swelling * e3[0, x]
 
-    @pl.loop(0, nx)
+    @pl.loop(0, nx, unroll=2)
     def _(x):
         mass = vol[x]
         swell = weighted(ring_sums(act_t, x), math.sqrt) + near(e3.at[0], x, 0, 0) * mass

time: 23.1 us -> 21.9 us (0.948)
  Pallas kernels: 21.1 us -> 19.9 us
    pallas_call x1, Pallas kernels: 21.1 us -> 19.9 us  [per_device(): pl.pallas_call(kernel, out_shape=(pltpu.VMEM(temp.shape, f32), pltpu.VMEM...]
where the time goes in v4:
time: 21.9 us; the launch traced here: 21.8 us
  Pallas kernels  19.9 us (91%)
  local copies, waits for them, and re-layouts  1.26 us (6%)
  between operations  0.64 us (3%)
    pallas_call x1, Pallas kernels, per_device(): pl.pallas_call(kernel, out_shape=(pltpu.VMEM(temp.shape, f32), pltpu.VMEM...  19.9 us
    unnamed x2, local copies, waits for them, and re-layouts  1.26 us

profile of v4, /device:TPU:1, one launch (start us, length us, event | category | flops | bytes accessed | tf_op | source)
XLA Modules:
  0.0 21.8 jit_solution(11990095174561168080)
XLA Ops:
  0.6 19.9 %shard_map.68 = (f32[8,8,128]{2,1,0:T(8,128)S(1)}, f32[3,8,8,128]{3,2,1,0:T(8,128)S(1)}) custom-call(f32[8,8,128]{2,1,0:T(8,128)} %temp_in.1, f32[8,8,128]{2,1,0:T(8,128)} %cond_in.1, f32[3,8,8,128]{3,2,1,0:T(8,128)} %shift_in.1, s32[64,128]{1,0:T(8,128)} %tally_in.1, s32[2,128]{1,0:T(2,128)} %sites_in.1), custom_call_target="tpu_custom_call" | custom-call | tf_op jit(solution)/shard_map/pallas_call | solution.py:467
  20.5 0.6 %copy.9 = f32[8,8,128]{2,1,0:T(8,128)} copy(f32[8,8,128]{2,1,0:T(8,128)S(1)} %get-tuple-element.2) | data formatting | bytes 65536
  21.2 0.6 %copy.10 = f32[3,8,8,128]{3,2,1,0:T(8,128)} copy(f32[3,8,8,128]{3,2,1,0:T(8,128)S(1)} %get-tuple-element.3) | data formatting | bytes 196608
